TPU v7x, 512 devices: a whole 4x4x16 slice. The times are simulated.
512 devices in a mesh: user: 8 (over x, core), seq: 64 (over z, y).
Axes of the slice: x: 4, y: 4, z: 16, core: 2. Of those that a mesh axis runs over, the one named last changes fastest.
Arguments:
- kv_cache: bfloat16 [16, 8192, 2, 2, 512], P('user', 'seq'), may hold values from -6 to 6
- spill_cache: bfloat16 [8, 4096, 2, 2, 512], P('user', 'seq'), may hold values from -6 to 6
- spill_owner: int32 [8, 64], P('user', 'seq'), may hold values from 0 to 1, as said below
- lengths: int32 [16], P('user'), may hold values from 2048 to 8192, as said below
- beam_tokens: int32 [16, 8, 4], P('user'), may hold values from 0 to 255
- codebook_embed: bfloat16 [4, 256, 512], P(None, 'user'), may hold values from -6 to 6
- w_query: bfloat16 [2, 512, 512], replicated, may hold values from -0.25 to 0.25
- w_gate: bfloat16 [2, 512, 512], replicated, may hold values from -0.25 to 0.25
- w_out: bfloat16 [2, 512, 512], replicated, may hold values from -0.25 to 0.25
Outputs:
- logits: float32 [16, 8, 4, 256], P('user')
Inputs may be any that keep to these rules, and one draw needn't show every extreme that they name: `lengths`: lengths lie between 2048 and 8192; some user has length 8192. `spill_owner`: each value names a user of the group, as an index 0 to 1.
All inputs are finite; a program needn't handle non-finite values.
Results may differ from a plain program's by a relative error of at most 0.011.
Values may be sent and summed in bfloat16 or wider, within the bound.
No kernel may reach another device: no remote copies, remote signals or barrier semaphores. Data moves between devices by JAX's collectives and lax.ppermute only.
A program may use at most 64 MiB of HBM per device.

v0:
```python
import jax
import jax.numpy as jnp
from jax import lax
from jax.sharding import PartitionSpec as P

D = 512
H = 8
LEVELS = 4
LAYERS = 2
BEAMS = 8


EPSILON = 1e-06


def normalize(values):
    return values * lax.rsqrt(jnp.mean(values * values, axis=-1, keepdims=True) + EPSILON)


def body(
    kv_cache, spill_cache, spill_owner, lengths, beam_tokens, codebook_embed, w_query, w_gate, w_out
):
    full_table = lax.all_gather(codebook_embed, "user", axis=1, tiled=True)
    seq_index = lax.axis_index("seq")
    user_count = kv_cache.shape[0]
    span = kv_cache.shape[1]
    head_size = D // H
    row_count = user_count * BEAMS
    code_count = full_table.shape[1]
    positions = seq_index * span + jnp.arange(span, dtype=jnp.int32)
    valid = positions[None, :] < lengths[:, None]
    owner_hit = jnp.arange(user_count, dtype=jnp.int32) == spill_owner[0, 0]
    tokens_flat = beam_tokens.reshape(row_count, LEVELS)
    stream = jnp.zeros((row_count, D), jnp.float32)
    results = []
    for level in range(LEVELS):
        onehot = (
            tokens_flat[:, level][:, None] == jnp.arange(code_count, dtype=jnp.int32)[None, :]
        ).astype(jnp.bfloat16)
        stream = stream + jnp.dot(onehot, full_table[level], preferred_element_type=jnp.float32)
        for layer in range(LAYERS):
            normed = normalize(stream).astype(jnp.bfloat16)
            queries = jnp.dot(normed, w_query[layer], preferred_element_type=jnp.float32).astype(
                jnp.bfloat16
            )
            gate_act = jax.nn.silu(
                jnp.dot(normed, w_gate[layer], preferred_element_type=jnp.float32)
            )
            query_heads = queries.reshape(user_count, BEAMS, H, head_size)
            key_heads = kv_cache[:, :, layer, 0].reshape(user_count, span, H, head_size)
            value_heads = kv_cache[:, :, layer, 1].reshape(user_count, span, H, head_size)
            scores = jnp.einsum(
                "ubhd,uphd->ubhp", query_heads, key_heads, preferred_element_type=jnp.float32
            ) * head_size ** (-0.5)
            weights_bf = jnp.where(valid[:, None, None, :], jax.nn.silu(scores), 0.0).astype(
                jnp.bfloat16
            )
            numerator = jnp.einsum(
                "ubhp,uphd->ubhd", weights_bf, value_heads, preferred_element_type=jnp.float32
            )
            owner_query = jnp.sum(
                jnp.where(owner_hit[:, None, None, None], query_heads.astype(jnp.float32), 0.0),
                axis=0,
            ).astype(jnp.bfloat16)
            spill_keys = spill_cache[0, :, layer, 0].reshape(-1, H, head_size)
            spill_values = spill_cache[0, :, layer, 1].reshape(-1, H, head_size)
            spill_scores = jnp.einsum(
                "bhd,phd->bhp", owner_query, spill_keys, preferred_element_type=jnp.float32
            ) * head_size ** (-0.5)
            spill_weights = jax.nn.silu(spill_scores).astype(jnp.bfloat16)
            spill_term = jnp.einsum(
                "bhp,phd->bhd", spill_weights, spill_values, preferred_element_type=jnp.float32
            )
            numerator = numerator + jnp.where(owner_hit[:, None, None, None], spill_term[None], 0.0)
            numerator = numerator.reshape(row_count, D)
            total = lax.psum(numerator, "seq")
            gated = (normalize(total) * gate_act).astype(jnp.bfloat16)
            stream = stream + jnp.dot(gated, w_out[layer], preferred_element_type=jnp.float32)
        final = normalize(stream).astype(jnp.bfloat16)
        results.append(
            jnp.dot(final, full_table[level].T, preferred_element_type=jnp.float32) * D ** (-0.5)
        )
    stacked = jnp.stack(results, axis=1)
    return stacked.reshape(user_count, BEAMS, LEVELS, code_count)


def solution(mesh):
    in_specs = (
        P("user", "seq", None, None, None),
        P("user", "seq", None, None, None),
        P("user", "seq"),
        P("user"),
        P("user", None, None),
        P(None, "user", None),
        P(),
        P(),
        P(),
    )
    out_specs = P("user", None, None, None)
    return jax.shard_map(body, mesh=mesh, in_specs=in_specs, out_specs=out_specs, check_vma=False)
```

profile of v0, /device:TPU:6, one launch (start us, length us, event | category | flops | bytes accessed | tf_op | source)
XLA Modules:
  0.0 2301.3 jit_solution(4197747357053335070)
XLA Ops:
  7.4 3.0 fusion.349
  17.6 26.1 %all-gather.2.cloned.1.call-done = bf16[4,256,512]{2,1,0:T(8,128)(2,1)} async-done(((bf16[4,32,512]{2,1,0:T(8,128)(2,1)}), bf16[4,256,512]{2,1,0:T(8,128)(2,1)}) %all-gather.2.cloned.1.call-update) | async-done | bytes 1048592 | tf_op jit(solution)/shard_map/all_gather | solution.py:23
  43.7 1.2 multiply_reduce_fusion.19
  46.7 279.7 %psum.56 = f32[16,512]{1,0:T(8,128)S(1)} all-reduce(f32[16,512]{1,0:T(8,128)S(1)} %reshape.261), channel_id=1, replica_groups=mesh['user'=8,'seq'=64] {'seq'}, use_global_device_ids=true, to_apply=%region_2.3 | all-reduce | flops 8192 | bytes 65536 | tf_op jit(solution)/shard_map/psum | solution.py:76
  326.6 1.7 multiply_reduce_fusion.17
  331.0 273.9 %psum.57 = f32[16,512]{1,0:T(8,128)S(1)} all-reduce(f32[16,512]{1,0:T(8,128)S(1)} %reshape.263), channel_id=1, replica_groups=mesh['user'=8,'seq'=64] {'seq'}, use_global_device_ids=true, to_apply=%region_6.7 | all-reduce | flops 8192 | bytes 65536 | tf_op jit(solution)/shard_map/psum | solution.py:76
  605.0 2.2 multiply_reduce_fusion.15
  608.6 1.3 convolution_bitcast_fusion.13
  611.8 273.9 %psum.58 = f32[16,512]{1,0:T(8,128)S(1)} all-reduce(f32[16,512]{1,0:T(8,128)S(1)} %reshape.265), channel_id=1, replica_groups=mesh['user'=8,'seq'=64] {'seq'}, use_global_device_ids=true, to_apply=%region_11.12 | all-reduce | flops 8192 | bytes 65536 | tf_op jit(solution)/shard_map/psum | solution.py:76
  886.5 2.3 multiply_reduce_fusion.12
  892.1 273.9 %psum.59 = f32[16,512]{1,0:T(8,128)S(1)} all-reduce(f32[16,512]{1,0:T(8,128)S(1)} %reshape.267), channel_id=1, replica_groups=mesh['user'=8,'seq'=64] {'seq'}, use_global_device_ids=true, to_apply=%region_15.16 | all-reduce | flops 8192 | bytes 65536 | tf_op jit(solution)/shard_map/psum | solution.py:76
  1166.1 2.3 multiply_reduce_fusion.10
  1169.5 1.3 select_reduce_fusion.3
  1170.9 1.9 convolution_bitcast_fusion.11
  1173.9 273.9 %psum.60 = f32[16,512]{1,0:T(8,128)S(1)} all-reduce(f32[16,512]{1,0:T(8,128)S(1)} %reshape.269), channel_id=1, replica_groups=mesh['user'=8,'seq'=64] {'seq'}, use_global_device_ids=true, to_apply=%region_20.21 | all-reduce | flops 8192 | bytes 65536 | tf_op jit(solution)/shard_map/psum | solution.py:76
  1448.6 1.7 multiply_reduce_fusion.7
  1453.9 273.9 %psum.61 = f32[16,512]{1,0:T(8,128)S(1)} all-reduce(f32[16,512]{1,0:T(8,128)S(1)} %reshape.271), channel_id=1, replica_groups=mesh['user'=8,'seq'=64] {'seq'}, use_global_device_ids=true, to_apply=%region_24.25 | all-reduce | flops 8192 | bytes 65536 | tf_op jit(solution)/shard_map/psum | solution.py:76
  1728.6 2.2 multiply_reduce_fusion.5
  1732.8 1.3 select_reduce_fusion.1
  1734.1 1.8 convolution_bitcast_fusion.9
  1737.2 273.9 %psum.62 = f32[16,512]{1,0:T(8,128)S(1)} all-reduce(f32[16,512]{1,0:T(8,128)S(1)} %reshape.273), channel_id=1, replica_groups=mesh['user'=8,'seq'=64] {'seq'}, use_global_device_ids=true, to_apply=%region_29.30 | all-reduce | flops 8192 | bytes 65536 | tf_op jit(solution)/shard_map/psum | solution.py:76
  2011.9 1.7 multiply_reduce_fusion.2
  2015.3 273.9 %psum.63 = f32[16,512]{1,0:T(8,128)S(1)} all-reduce(f32[16,512]{1,0:T(8,128)S(1)} %reshape.275), channel_id=1, replica_groups=mesh['user'=8,'seq'=64] {'seq'}, use_global_device_ids=true, to_apply=%region_33.34 | all-reduce | flops 8192 | bytes 65536 | tf_op jit(solution)/shard_map/psum | solution.py:76
  2289.3 1.5 multiply_reduce_fusion
  (178 shorter events, 35.7 us)
Async XLA Ops:
  6.5 37.2 %all-gather.2.cloned.1.call-start = ((), (), s32[]{:S(2)}) async-start(), calls=%async_computation | async-start | bytes 1179648 | tf_op jit(solution)/shard_map/all_gather | solution.py:23
  6.5 0.7 copy-start.19
  10.8 1.0 copy-start.2
  15.1 29.9 %copy-start = (bf16[2,512,512]{2,1,0:T(8,128)(2,1)S(1)}, bf16[2,512,512]{2,1,0:T(8,128)(2,1)}, u32[]{:S(2)}) copy-start(bf16[2,512,512]{2,1,0:T(8,128)(2,1)} %param.15) | copy-start | bytes 3145732
  16.2 873.7 %copy-start.3 = (bf16[64,8,64]{2,1,0:T(8,128)(2,1)}, bf16[64,8,64]{2,1,0:T(8,128)(2,1)S(1)}, u32[]{:S(2)}) copy-start(bf16[64,8,64]{2,1,0:T(8,128)(2,1)S(1)} %reshape_squeeze.22) | copy-start | bytes 196612
  16.2 874.6 %copy-start.14 = (pred[2]{0:T(512)(128)(4,1)}, pred[2]{0:T(512)(128)(4,1)S(1)}, u32[]{:S(2)}) copy-start(pred[2]{0:T(512)(128)(4,1)S(1)} %iota_compare_fusion.8) | copy-start | bytes 10
  16.2 0.7 copy-start.26
  17.0 312.0 %copy-start.27 = (pred[2,128]{1,0:T(4,128)(4,1)}, pred[2,128]{1,0:T(4,128)(4,1)S(1)}, u32[]{:S(2)}) copy-start(pred[2,128]{1,0:T(4,128)(4,1)S(1)} %broadcast_compare_fusion) | copy-start | bytes 772
  45.0 0.9 copy-start.6
  45.0 1.0 copy-start.9
  329.0 278.2 %copy-start.1 = (bf16[4,256,512]{2,1,0:T(8,128)(2,1)S(1)}, bf16[4,256,512]{2,1,0:T(8,128)(2,1)}, u32[]{:S(2)}) copy-start(bf16[4,256,512]{2,1,0:T(8,128)(2,1)} %all-gather.2.cloned.1.call-done) | copy-start | bytes 3145732
  608.6 1.3 copy-start.28
  885.7 0.8 copy-start.13
  1169.2 1.6 copy-start.7
  1170.9 1.9 copy-start.15
  1170.9 1.9 copy-start.29
  1450.9 0.9 copy-start.4
  1727.9 0.8 copy-start.18
  1732.5 1.6 copy-start.8
  1734.1 1.8 copy-start.16
  1734.1 1.8 copy-start.30
  2011.1 0.8 copy-start.11
  2013.6 0.9 copy-start.5
  2013.8 275.5 %copy-start.25 = (bf16[2,512,512]{2,1,0:T(8,128)(2,1)S(1)}, bf16[2,512,512]{2,1,0:T(8,128)(2,1)}, u32[]{:S(2)}) copy-start(bf16[2,512,512]{2,1,0:T(8,128)(2,1)} %param.17) | copy-start | bytes 3145732
  (12 other events, 7.5 us)
Sparse Core Ops, SparseCore 0:
  9.5 34.1 all-gather.1
where the time goes:
time: 2300 us
  blocking collectives  2200 us (96%)
  matrix products  35.2 us (2%)
  waiting for transfers between devices  26.9 us (1%)
    psum x8, blocking collectives, body(): total = lax.psum(numerator, 'seq')  2200 us
  transfers between devices with their start and end apart: 1, of which 1 were waited for; matrix products, arithmetic and copies ran while one was open for 0% of the time, Pallas kernels for 0%

commit v1 on v0

v1 whole, which is shorter than its diff:
```python
import functools

import jax
import jax.numpy as jnp
from jax import lax
from jax.experimental import pallas as pl
from jax.experimental.pallas import tpu as pltpu
from jax.sharding import Mesh, PartitionSpec as P

D = 512
H = 8
V = 256
LEVELS = 4
LAYERS = 2
BEAMS = 8
U_DEV = 2
NX, NC, NZ, NY = 4, 2, 16, 4
GROUPS = NX * NC
PLANE = NX * NC * NY
COLS = D // NX
HEAD = D // H
EPSILON = 1e-06
PLANE_AXES = ("x", "core", "y")
USER_AXES = ("x", "core")

bf16 = jnp.bfloat16
f32 = jnp.float32


def normalize(values):
    return values * lax.rsqrt(jnp.mean(values * values, axis=-1, keepdims=True) + EPSILON)


def silu(values):
    return values / (1.0 + jnp.exp(-values))


def finish_layer(recv_ref, stream_ref, gate_ref, wo_ref):
    sums = jnp.sum(recv_ref[...].reshape(NX, NC * NY, BEAMS, COLS), axis=1)
    total = jnp.concatenate([sums[i] for i in range(NX)], axis=-1)
    gated = (normalize(total) * gate_ref[...]).astype(bf16)
    return stream_ref[...] + jnp.dot(gated, wo_ref[...], preferred_element_type=f32)


def begin_layer(stream, kv_ref, wq_ref, wg_ref, out_ref, gate_out):
    normed = normalize(stream).astype(bf16)
    query = jnp.dot(normed, wq_ref[...], preferred_element_type=f32)
    gate_out[...] = silu(jnp.dot(normed, wg_ref[...], preferred_element_type=f32))
    low = lax.broadcasted_iota(jnp.int32, (BEAMS, COLS), 1) < HEAD
    pair = jnp.concatenate([jnp.where(low, query, 0.0), jnp.where(low, 0.0, query)], axis=0)
    keys = kv_ref[:, 0].reshape(-1, COLS)
    values = kv_ref[:, 1].reshape(-1, COLS)
    scores = lax.dot_general(
        pair.astype(bf16), keys, (((1,), (1,)), ((), ())), preferred_element_type=f32
    ) * HEAD ** (-0.5)
    weights = silu(scores).astype(bf16)
    part = jnp.dot(weights, values, preferred_element_type=f32)
    mine = jnp.where(low, part[:BEAMS], part[BEAMS:])
    out_ref[...] = jnp.broadcast_to(mine[None], (PLANE, BEAMS, COLS))


def first_kernel(emb_ref, kv_ref, wq_ref, wg_ref, out_ref, stream_out, gate_out):
    stream = emb_ref[...]
    stream_out[...] = stream
    begin_layer(stream, kv_ref, wq_ref, wg_ref, out_ref, gate_out)


def middle_kernel(recv_ref, stream_ref, gate_ref, wo_ref, kv_ref, wq_ref, wg_ref, out_ref, stream_out, gate_out):
    stream = finish_layer(recv_ref, stream_ref, gate_ref, wo_ref)
    stream_out[...] = stream
    begin_layer(stream, kv_ref, wq_ref, wg_ref, out_ref, gate_out)


def level_logits(stream, table_ref):
    final = normalize(stream).astype(bf16)
    return lax.dot_general(
        final, table_ref[...], (((1,), (1,)), ((), ())), preferred_element_type=f32
    ) * D ** (-0.5)


def turn_kernel(recv_ref, stream_ref, gate_ref, wo_ref, kv_ref, wq_ref, wg_ref, emb_ref, table_ref,
                out_ref, stream_out, gate_out, logits_out):
    stream = finish_layer(recv_ref, stream_ref, gate_ref, wo_ref)
    logits_out[...] = level_logits(stream, table_ref)
    stream = stream + emb_ref[...]
    stream_out[...] = stream
    begin_layer(stream, kv_ref, wq_ref, wg_ref, out_ref, gate_out)


def last_kernel(recv_ref, stream_ref, gate_ref, wo_ref, table_ref, logits_out):
    stream = finish_layer(recv_ref, stream_ref, gate_ref, wo_ref)
    logits = level_logits(stream, table_ref)
    logits_out[...] = jnp.broadcast_to(logits[None], (NZ, BEAMS, V))


VMEM = pl.BlockSpec(memory_space=pltpu.VMEM)


def call(kernel, args, outs):
    return pl.pallas_call(
        kernel,
        in_specs=[VMEM] * len(args),
        out_specs=[VMEM] * len(outs),
        out_shape=[jax.ShapeDtypeStruct(shape, f32) for shape in outs],
        compiler_params=pltpu.CompilerParams(vmem_limit_bytes=32 * 1024 * 1024),
    )(*args)


STEP_OUTS = [(PLANE, BEAMS, COLS), (BEAMS, D), (BEAMS, D)]


def body(
    kv_cache, spill_cache, spill_owner, lengths, beam_tokens, codebook_embed, w_query, w_gate, w_out
):
    xi, ci = lax.axis_index("x"), lax.axis_index("core")
    zi, yi = lax.axis_index("z"), lax.axis_index("y")
    span = kv_cache.shape[1]
    spill = spill_cache.shape[1]

    table = lax.all_gather(codebook_embed, USER_AXES, axis=1, tiled=True)
    tokens = lax.all_gather(beam_tokens, USER_AXES, axis=0, tiled=True)

    positions = (zi * NY + yi) * span + jnp.arange(span, dtype=jnp.int32)
    valid = positions[None, :] < lengths[:, None]
    owned = jnp.arange(U_DEV, dtype=jnp.int32) == spill_owner[0, 0]
    keep = jnp.concatenate(
        [valid.reshape(U_DEV, NC, span // NC), jnp.broadcast_to(owned[:, None, None], (U_DEV, NC, spill // NC))],
        axis=2,
    )
    resident = kv_cache.reshape(U_DEV, NC, span // NC, LAYERS, 2, NX, COLS)
    extra = jnp.broadcast_to(
        spill_cache.reshape(1, NC, spill // NC, LAYERS, 2, NX, COLS),
        (U_DEV, NC, spill // NC, LAYERS, 2, NX, COLS),
    )
    memory = jnp.concatenate([resident, extra], axis=2)
    is_value = jnp.arange(2) == 1
    memory = jnp.where(
        keep[:, :, :, None, None, None, None] | is_value[None, None, None, None, :, None, None],
        memory,
        jnp.zeros((), bf16),
    )
    memory = memory.transpose(5, 1, 0, 3, 4, 2, 6)
    share = memory.shape[5]
    memory = memory.reshape(GROUPS, U_DEV, LAYERS, 2, share, COLS)
    memory = lax.all_to_all(memory, USER_AXES, 0, 0, tiled=True)
    memory = memory.reshape(NZ, LAYERS, 2, share, COLS)
    memory = lax.all_to_all(memory, "z", 0, 0, tiled=True)
    kv = [memory[:, layer] for layer in range(LAYERS)]

    mine = lax.dynamic_index_in_dim(tokens, zi, 0, keepdims=False)
    onehot = (mine.T[:, :, None] == jnp.arange(V, dtype=jnp.int32)[None, None, :]).astype(bf16)
    embeds = jnp.einsum("tbv,tvd->tbd", onehot, table, preferred_element_type=f32)

    wq = [lax.dynamic_slice(w_query[layer], (0, xi * COLS), (D, COLS)) for layer in range(LAYERS)]
    wg = [w_gate[layer] for layer in range(LAYERS)]
    wo = [w_out[layer] for layer in range(LAYERS)]

    def exchange(parts):
        return lax.all_to_all(parts, PLANE_AXES, 0, 0, tiled=True)

    early = []
    for level in range(LEVELS):
        if level == 0:
            parts, stream, gate = call(first_kernel, (embeds[0], kv[0], wq[0], wg[0]), STEP_OUTS)
        else:
            parts, stream, gate, logits = call(
                turn_kernel,
                (recv, stream, gate, wo[1], kv[0], wq[0], wg[0], embeds[level], table[level - 1]),
                STEP_OUTS + [(BEAMS, V)],
            )
            early.append(logits)
        recv = exchange(parts)
        parts, stream, gate = call(
            middle_kernel, (recv, stream, gate, wo[0], kv[1], wq[1], wg[1]), STEP_OUTS
        )
        recv = exchange(parts)
    (final,) = call(last_kernel, (recv, stream, gate, wo[1], table[LEVELS - 1]), [(NZ, BEAMS, V)])
    last = lax.all_to_all(final, "z", 0, 0, tiled=True)
    group = xi * NC + ci
    pieces = [
        lax.dynamic_slice_in_dim(lax.all_gather(value, "z", axis=0), group * U_DEV, U_DEV, 0)
        for value in early
    ]
    pieces.append(lax.dynamic_slice_in_dim(last, group * U_DEV, U_DEV, 0))
    return jnp.stack(pieces, axis=2)


def solution(mesh):
    inner = Mesh(mesh.devices.reshape(NX, NC, NZ, NY), ("x", "core", "z", "y"))
    users, seq = ("x", "core"), ("z", "y")
    in_specs = (
        P(users, seq, None, None, None),
        P(users, seq, None, None, None),
        P(users, seq),
        P(users),
        P(users, None, None),
        P(None, users, None),
        P(),
        P(),
        P(),
    )
    out_specs = P(users, None, None, None)
    return jax.shard_map(body, mesh=inner, in_specs=in_specs, out_specs=out_specs, check_vma=False)
```

time: 2300 us -> 342 us (0.15)
  blocking collectives: 2200 us -> 187 us
  waiting for transfers between devices: 26.9 us -> 70.3 us
  starting transfers between devices: 0.01 us -> 36.7 us
  matrix products: 35.2 us -> 1.49 us
    psum x8 -> x0, blocking collectives: 2200 us -> none  [body(): total = lax.psum(numerator, 'seq')]
    all_gather x0 -> x4, blocking collectives: none -> 102 us  [the longest x3 88.8 us: body(): lax.all_gather(value, 'z', axis=0)]
    all_to_all x0 -> x6, blocking collectives: none -> 85.5 us  [the longest x5 57.5 us: exchange(): return lax.all_to_all(parts, PLANE_AXES, 0, 0, tiled=True)]
    all_to_all x0 -> x5, waiting for transfers between devices: none -> 50.5 us  [the longest x1 38.1 us: body(): memory = lax.all_to_all(memory, 'z', 0, 0, tiled=True)]
    all_to_all x0 -> x5, starting transfers between devices: none -> 36.6 us  [the longest x3 18.9 us: exchange(): return lax.all_to_all(parts, PLANE_AXES, 0, 0, tiled=True)]
    dot_general x40 -> x1, matrix products: 35.2 us -> 1.49 us  [body(): jnp.einsum('tbv,tvd->tbd', onehot, table, preferred_element_type=f32)]
  transfers between devices with their start and end apart: 1 -> 6, of which waited for: 1 -> 5; matrix products, arithmetic and copies ran while one was open for 0% -> 2% of each run, Pallas kernels for 0% -> 0%
where the time goes in v1:
time: 342 us; the launch traced here: 340 us
  blocking collectives  187 us (55%)
  waiting for transfers between devices  70.3 us (21%)
  starting transfers between devices  36.7 us (11%)
  local copies, waits for them, and re-layouts  20.7 us (6%)
  between operations  14.5 us (4%)
  Pallas kernels  8.56 us (3%)
    all_gather x3, blocking collectives, body(): lax.all_gather(value, 'z', axis=0)  88.8 us
    all_to_all x5, blocking collectives, exchange(): return lax.all_to_all(parts, PLANE_AXES, 0, 0, tiled=True)  57.5 us
    all_to_all x1, waiting for transfers between devices, body(): memory = lax.all_to_all(memory, 'z', 0, 0, tiled=True)  38.1 us
    all_to_all x1, blocking collectives, body(): memory = lax.all_to_all(memory, USER_AXES, 0, 0, tiled=True)  28 us
    all_gather x1, waiting for transfers between devices, body(): table = lax.all_gather(codebook_embed, USER_AXES, axis=1, tiled=True)  19.2 us
    all_to_all x3, starting transfers between devices, exchange(): return lax.all_to_all(parts, PLANE_AXES, 0, 0, tiled=True)  18.9 us
    all_gather x1, blocking collectives, body(): tokens = lax.all_gather(beam_tokens, USER_AXES, axis=0, tiled=True)  12.8 us
    all_to_all x3, waiting for transfers between devices, exchange(): return lax.all_to_all(parts, PLANE_AXES, 0, 0, tiled=True)  12.4 us
  transfers between devices with their start and end apart: 6, of which 5 were waited for; matrix products, arithmetic and copies ran while one was open for 2% of the time, Pallas kernels for 0%

profile of v1, /device:TPU:6, one launch (start us, length us, event | category | flops | bytes accessed | tf_op | source)
XLA Modules:
  0.0 340.2 jit_solution(10345611465318535848)
XLA Ops:
  10.5 28.0 %all_to_all.55 = bf16[8,2,2,2,96,128]{5,4,3,1,2,0:T(8,128)(2,1)S(1)} all-to-all(bf16[8,2,2,2,96,128]{5,4,3,1,2,0:T(8,128)(2,1)S(1)} %bitcast.58), channel_id=1, replica_groups=mesh['x'=4,'core'=2,'z'=16,'y'=4] {'x','core'}, dimensions={0} | all-to-all | bytes 3145728 | tf_op jit(solution)/shard_map/all_to_all | solution.py:145
  39.8 11.7 %all-to-all-start.1 = ((bf16[16,2,2,96,128]{4,3,2,1,0:T(8,128)(2,1)}), bf16[16,2,2,96,128]{4,3,2,1,0:T(8,128)(2,1)}, u32[]{:S(2)}, u32[]{:S(2)}) async-start(bf16[16,2,2,96,128]{4,3,2,1,0:T(8,128)(2,1)} %bitcast.6), calls=%async_computation.1 | async-start | bytes 3145728 | tf_op jit(solution)/shard_map/all_to_all | solution.py:147
  52.2 12.8 %all_gather.24 = s32[16,8,4]{1,2,0:T(4,128)S(1)} all-gather(s32[2,8,4]{1,2,0:T(4,128)S(1)} %copy-done.22), channel_id=1, replica_groups=mesh['x'=4,'core'=2,'z'=16,'y'=4] {'x','core'}, dimensions={0}, use_global_device_ids=true | all-gather | bytes 2304 | tf_op jit(solution)/shard_map/all_gather | solution.py:121
  66.0 19.2 %all-gather.5.cloned.1.call-done = bf16[4,256,512]{2,1,0:T(8,128)(2,1)} async-done(((bf16[4,32,512]{2,1,0:T(8,128)(2,1)}), bf16[4,256,512]{2,1,0:T(8,128)(2,1)}) %all-gather.5.cloned.1.call-update) | async-done | bytes 1048592 | tf_op jit(solution)/shard_map/all_gather | solution.py:120
  85.2 1.5 fusion
  87.3 38.1 %all-to-all-done.1 = bf16[16,2,2,96,128]{4,3,2,1,0:T(8,128)(2,1)} async-done(((bf16[16,2,2,96,128]{4,3,2,1,0:T(8,128)(2,1)}), bf16[16,2,2,96,128]{4,3,2,1,0:T(8,128)(2,1)}, u32[]{:S(2)}, u32[]{:S(2)}) %all-to-all-start.1) | async-done | bytes 1572896 | tf_op jit(solution)/shard_map/all_to_all | solution.py:147
  125.4 1.5 slice_bitcast_fusion
  128.7 7.3 %all-to-all-start.2 = ((f32[32,8,128]{2,1,0:T(8,128)}), f32[32,8,128]{2,1,0:T(8,128)S(1)}, u32[]{:S(2)}, u32[]{:S(2)}) async-start(f32[32,8,128]{2,1,0:T(8,128)} %get-tuple-element.32), calls=%async_computation.2 | async-start | bytes 262144 | tf_op jit(solution)/shard_map/all_to_all | solution.py:159
  136.1 2.1 slice_bitcast_fusion.2
  139.0 2.9 all-to-all-done.2.recv_ref
  147.1 5.8 %all-to-all-start.3 = ((f32[32,8,128]{2,1,0:T(8,128)}), f32[32,8,128]{2,1,0:T(8,128)S(1)}, u32[]{:S(2)}, u32[]{:S(2)}) async-start(f32[32,8,128]{2,1,0:T(8,128)} %copy-done.6), calls=%async_computation.3 | async-start | bytes 262144 | tf_op jit(solution)/shard_map/all_to_all | solution.py:159
  152.8 2.2 slice_bitcast_fusion.6
  155.1 3.6 %all-to-all-done.3.recv_ref = f32[32,8,128]{2,1,0:T(8,128)S(1)} async-done(((f32[32,8,128]{2,1,0:T(8,128)}), f32[32,8,128]{2,1,0:T(8,128)S(1)}, u32[]{:S(2)}, u32[]{:S(2)}) %all-to-all-start.3) | async-done | bytes 131104 | tf_op jit(solution)/shard_map/all_to_all | solution.py:159
  162.7 11.6 %all_to_all.56.recv_ref = f32[32,8,128]{2,1,0:T(8,128)S(1)} all-to-all(f32[32,8,128]{2,1,0:T(8,128)S(1)} %get-tuple-element.39), channel_id=1, replica_groups=mesh['x'=4,'core'=2,'z'=16,'y'=4] {'x','core','y'}, dimensions={0} | all-to-all | bytes 262144 | tf_op jit(solution)/shard_map/all_to_all | solution.py:159
  175.1 11.4 %all_to_all.57.recv_ref = f32[32,8,128]{2,1,0:T(8,128)S(1)} all-to-all(f32[32,8,128]{2,1,0:T(8,128)S(1)} %get-tuple-element.42), channel_id=1, replica_groups=mesh['x'=4,'core'=2,'z'=16,'y'=4] {'x','core','y'}, dimensions={0} | all-to-all | bytes 262144 | tf_op jit(solution)/shard_map/all_to_all | solution.py:159
  187.4 11.5 %all_to_all.58.recv_ref = f32[32,8,128]{2,1,0:T(8,128)S(1)} all-to-all(f32[32,8,128]{2,1,0:T(8,128)S(1)} %get-tuple-element.46), channel_id=1, replica_groups=mesh['x'=4,'core'=2,'z'=16,'y'=4] {'x','core','y'}, dimensions={0} | all-to-all | bytes 262144 | tf_op jit(solution)/shard_map/all_to_all | solution.py:159
  199.7 11.4 %all_to_all.59.recv_ref = f32[32,8,128]{2,1,0:T(8,128)S(1)} all-to-all(f32[32,8,128]{2,1,0:T(8,128)S(1)} %get-tuple-element.49), channel_id=1, replica_groups=mesh['x'=4,'core'=2,'z'=16,'y'=4] {'x','core','y'}, dimensions={0} | all-to-all | bytes 262144 | tf_op jit(solution)/shard_map/all_to_all | solution.py:159
  212.0 11.5 %all_to_all.60.recv_ref = f32[32,8,128]{2,1,0:T(8,128)S(1)} all-to-all(f32[32,8,128]{2,1,0:T(8,128)S(1)} %get-tuple-element.53), channel_id=1, replica_groups=mesh['x'=4,'core'=2,'z'=16,'y'=4] {'x','core','y'}, dimensions={0} | all-to-all | bytes 262144 | tf_op jit(solution)/shard_map/all_to_all | solution.py:159
  224.9 5.8 %all-to-all-start.9 = ((f32[32,8,128]{2,1,0:T(8,128)}), f32[32,8,128]{2,1,0:T(8,128)S(1)}, u32[]{:S(2)}, u32[]{:S(2)}) async-start(f32[32,8,128]{2,1,0:T(8,128)} %get-tuple-element.56), calls=%async_computation.9 | async-start | bytes 262144 | tf_op jit(solution)/shard_map/all_to_all | solution.py:159
  230.7 5.8 %all-to-all-done.9.recv_ref = f32[32,8,128]{2,1,0:T(8,128)S(1)} async-done(((f32[32,8,128]{2,1,0:T(8,128)}), f32[32,8,128]{2,1,0:T(8,128)S(1)}, u32[]{:S(2)}, u32[]{:S(2)}) %all-to-all-start.9) | async-done | bytes 131104 | tf_op jit(solution)/shard_map/all_to_all | solution.py:159
  237.7 6.1 %all-to-all-start.10 = ((f32[16,8,256]{2,1,0:T(8,128)}), f32[16,8,256]{2,1,0:T(8,128)S(1)}, u32[]{:S(2)}, u32[]{:S(2)}) async-start(f32[16,8,256]{2,1,0:T(8,128)} %shard_map.99), calls=%async_computation.10 | async-start | bytes 262144 | tf_op jit(solution)/shard_map/all_to_all | solution.py:178
  243.8 32.3 %all-gather = f32[128,256]{1,0:T(8,128)S(1)} all-gather(f32[8,256]{1,0:T(8,128)S(1)} %copy-done.18), channel_id=2, replica_groups=mesh['x'=4,'core'=2,'z'=16,'y'=4] {'z'}, dimensions={0}, use_global_device_ids=true | all-gather | bytes 139264 | tf_op jit(solution)/shard_map/all_gather | solution.py:181
  276.1 27.6 %all-gather.1 = f32[128,256]{1,0:T(8,128)S(1)} all-gather(f32[8,256]{1,0:T(8,128)S(1)} %get-tuple-element.45), channel_id=3, replica_groups=mesh['x'=4,'core'=2,'z'=16,'y'=4] {'z'}, dimensions={0}, use_global_device_ids=true | all-gather | bytes 139264 | tf_op jit(solution)/shard_map/all_gather | solution.py:181
  303.8 28.9 %all-gather.2 = f32[128,256]{1,0:T(8,128)S(1)} all-gather(f32[8,256]{1,0:T(8,128)S(1)} %get-tuple-element.52), channel_id=4, replica_groups=mesh['x'=4,'core'=2,'z'=16,'y'=4] {'z'}, dimensions={0}, use_global_device_ids=true | all-gather | bytes 139264 | tf_op jit(solution)/shard_map/all_gather | solution.py:181
  (86 shorter events, 25.0 us)
Async XLA Ops:
  6.5 2.0 copy-start.19
  8.5 1.0 copy-start.23
  39.8 12.4 %copy-start.22 = (s32[2,8,4]{1,2,0:T(4,128)S(1)}, s32[2,8,4]{1,2,0:T(4,128)}, u32[]{:S(2)}) copy-start(s32[2,8,4]{1,2,0:T(4,128)} %param.13) | copy-start | bytes 772
  39.8 25.2 %copy-start.20 = (bf16[2,512,512]{2,1,0:T(8,128)(2,1)S(1)}, bf16[2,512,512]{2,1,0:T(8,128)(2,1)}, u32[]{:S(2)}) copy-start(bf16[2,512,512]{2,1,0:T(8,128)(2,1)} %param.15) | copy-start | bytes 3145732
  39.8 85.6 %all-to-all-start.1 = ((bf16[16,2,2,96,128]{4,3,2,1,0:T(8,128)(2,1)}), bf16[16,2,2,96,128]{4,3,2,1,0:T(8,128)(2,1)}, u32[]{:S(2)}, u32[]{:S(2)}) async-start(bf16[16,2,2,96,128]{4,3,2,1,0:T(8,128)(2,1)} %bitcast.6), calls=%async_computation.1 | async-start | bytes 3145728 | tf_op jit(solution)/shard_map/all_to_all | solution.py:147
  51.5 14.5 %copy-start.21 = (bf16[2,512,512]{2,1,0:T(8,128)(2,1)S(1)}, bf16[2,512,512]{2,1,0:T(8,128)(2,1)}, u32[]{:S(2)}) copy-start(bf16[2,512,512]{2,1,0:T(8,128)(2,1)} %param.16) | copy-start | bytes 3145732
  51.5 33.7 %all-gather.5.cloned.1.call-start = ((), (), s32[]{:S(2)}) async-start(), calls=%async_computation.11 | async-start | bytes 1179648 | tf_op jit(solution)/shard_map/all_gather | solution.py:120
  128.7 9.4 %copy-start.15 = (f32[8,512]{1,0:T(8,128)}, f32[8,512]{1,0:T(8,128)S(1)}, u32[]{:S(2)}) copy-start(f32[8,512]{1,0:T(8,128)S(1)} %get-tuple-element.34.gate_ref) | copy-start | bytes 49156
  128.7 13.2 %all-to-all-start.2 = ((f32[32,8,128]{2,1,0:T(8,128)}), f32[32,8,128]{2,1,0:T(8,128)S(1)}, u32[]{:S(2)}, u32[]{:S(2)}) async-start(f32[32,8,128]{2,1,0:T(8,128)} %get-tuple-element.32), calls=%async_computation.2 | async-start | bytes 262144 | tf_op jit(solution)/shard_map/all_to_all | solution.py:159
  142.0 1.0 copy-start
  143.0 0.7 copy-start.14
  143.7 0.7 copy-start.16
  147.1 11.6 %all-to-all-start.3 = ((f32[32,8,128]{2,1,0:T(8,128)}), f32[32,8,128]{2,1,0:T(8,128)S(1)}, u32[]{:S(2)}, u32[]{:S(2)}) async-start(f32[32,8,128]{2,1,0:T(8,128)} %copy-done.6), calls=%async_computation.3 | async-start | bytes 262144 | tf_op jit(solution)/shard_map/all_to_all | solution.py:159
  158.7 15.6 %copy-start.1 = (bf16[512,512]{1,0:T(8,128)(2,1)S(1)}, bf16[512,512]{1,0:T(8,128)(2,1)}, u32[]{:S(2)}) copy-start(bf16[512,512]{1,0:T(8,128)(2,1)} %get-tuple-element.66.wo_ref) | copy-start | bytes 1572868
  158.7 1.0 copy-start.4
  159.7 0.7 copy-start.8
  162.7 11.6 %copy-start.17 = (f32[8,256]{1,0:T(8,128)}, f32[8,256]{1,0:T(8,128)S(1)}, u32[]{:S(2)}) copy-start(f32[8,256]{1,0:T(8,128)S(1)} %get-tuple-element.38) | copy-start | bytes 24580
  162.7 23.8 %copy-start.3 = (bf16[256,512]{1,0:T(8,128)(2,1)S(1)}, bf16[256,512]{1,0:T(8,128)(2,1)}, u32[]{:S(2)}) copy-start(bf16[256,512]{1,0:T(8,128)(2,1)} %get-tuple-element.63.table_ref) | copy-start | bytes 786436
  162.7 23.8 %copy-start.7 = (f32[8,512]{1,0:T(8,128)S(1)}, f32[8,512]{1,0:T(8,128)}, u32[]{:S(2)}) copy-start(f32[8,512]{1,0:T(8,128)} %get-tuple-element.72.emb_ref) | copy-start | bytes 49156
  187.4 23.7 %copy-start.2 = (bf16[256,512]{1,0:T(8,128)(2,1)S(1)}, bf16[256,512]{1,0:T(8,128)(2,1)}, u32[]{:S(2)}) copy-start(bf16[256,512]{1,0:T(8,128)(2,1)} %get-tuple-element.62.table_ref) | copy-start | bytes 786436
  211.9 24.6 %copy-start.5 = (bf16[256,512]{1,0:T(8,128)(2,1)S(1)}, bf16[256,512]{1,0:T(8,128)(2,1)}, u32[]{:S(2)}) copy-start(bf16[256,512]{1,0:T(8,128)(2,1)} %get-tuple-element.61.table_ref) | copy-start | bytes 786436
  223.5 20.3 %copy-start.18 = (f32[8,256]{1,0:T(8,128)S(1)}, f32[8,256]{1,0:T(8,128)}, u32[]{:S(2)}) copy-start(f32[8,256]{1,0:T(8,128)} %copy-done.17) | copy-start | bytes 24580
  224.9 11.6 %all-to-all-start.9 = ((f32[32,8,128]{2,1,0:T(8,128)}), f32[32,8,128]{2,1,0:T(8,128)S(1)}, u32[]{:S(2)}, u32[]{:S(2)}) async-start(f32[32,8,128]{2,1,0:T(8,128)} %get-tuple-element.56), calls=%async_computation.9 | async-start | bytes 262144 | tf_op jit(solution)/shard_map/all_to_all | solution.py:159
  237.7 95.0 %all-to-all-start.10 = ((f32[16,8,256]{2,1,0:T(8,128)}), f32[16,8,256]{2,1,0:T(8,128)S(1)}, u32[]{:S(2)}, u32[]{:S(2)}) async-start(f32[16,8,256]{2,1,0:T(8,128)} %shard_map.99), calls=%async_computation.10 | async-start | bytes 262144 | tf_op jit(solution)/shard_map/all_to_all | solution.py:178
  (6 other events, 3.9 us)
Sparse Core Ops, SparseCore 0:
  54.5 30.6 all-gather.4

commit v2 on v1

v2 whole, which is shorter than its diff:
```python
import functools

import jax
import jax.numpy as jnp
from jax import lax
from jax.experimental import pallas as pl
from jax.experimental.pallas import tpu as pltpu
from jax.sharding import Mesh, PartitionSpec as P

D = 512
H = 8
V = 256
LEVELS = 4
LAYERS = 2
BEAMS = 8
U_DEV = 2
NX, NC, NQ, NL, NY = 4, 2, 4, 4, 4
AREA = NC * NL * NY
COLS = D // NC
HEAD = D // H
HEADS = COLS // HEAD
EPSILON = 1e-06
AREA_AXES = ("core", "zl", "y")
USER_AXES = ("x", "core")
Z_AXES = ("quad", "zl")
RINGS = [[NL * q + (i if q in (0, 3) else NL - 1 - i) for q in range(NQ)] for i in range(NL)]

bf16 = jnp.bfloat16
f32 = jnp.float32


def normalize(values):
    return values * lax.rsqrt(jnp.mean(values * values, axis=-1, keepdims=True) + EPSILON)


def silu(values):
    return values / (1.0 + jnp.exp(-values))


def finish_layer(layer, recv_ref, stream_ref, gate_ref, wo_ref):
    parts = recv_ref[...].astype(f32).reshape(NC, NL * NY, BEAMS, COLS)
    sums = jnp.sum(parts, axis=1)
    total = jnp.concatenate([sums[i] for i in range(NC)], axis=-1)
    gated = (normalize(total) * gate_ref[...]).astype(bf16)
    return stream_ref[...] + jnp.dot(gated, wo_ref[layer], preferred_element_type=f32)


def begin_layer(layer, stream, kv_ref, wq_ref, wg_ref, out_ref, gate_out):
    normed = normalize(stream).astype(bf16)
    query = jnp.dot(normed, wq_ref[layer], preferred_element_type=f32)
    gate_out[...] = silu(jnp.dot(normed, wg_ref[layer], preferred_element_type=f32))
    head_of = lax.broadcasted_iota(jnp.int32, (BEAMS, COLS), 1) // HEAD
    spread = jnp.concatenate([jnp.where(head_of == h, query, 0.0) for h in range(HEADS)], axis=0)
    keys = kv_ref[:, layer, 0].reshape(-1, COLS)
    values = kv_ref[:, layer, 1].reshape(-1, COLS)
    scores = lax.dot_general(
        spread.astype(bf16), keys, (((1,), (1,)), ((), ())), preferred_element_type=f32
    ) * HEAD ** (-0.5)
    weights = silu(scores).astype(bf16)
    part = jnp.dot(weights, values, preferred_element_type=f32)
    mine = jnp.zeros((BEAMS, COLS), f32)
    for h in range(HEADS):
        mine = jnp.where(head_of == h, part[h * BEAMS:(h + 1) * BEAMS], mine)
    copies = jnp.broadcast_to(mine[None], (AREA, BEAMS, COLS)).reshape(AREA * BEAMS, COLS)
    out_ref[...] = copies.astype(bf16)


def level_logits(level, stream, table_ref):
    final = normalize(stream).astype(bf16)
    return lax.dot_general(
        final, table_ref[level], (((1,), (1,)), ((), ())), preferred_element_type=f32
    ) * D ** (-0.5)


def first_kernel(emb_ref, kv_ref, wq_ref, wg_ref, out_ref, stream_out, gate_out):
    stream = emb_ref[0]
    stream_out[...] = stream
    begin_layer(0, stream, kv_ref, wq_ref, wg_ref, out_ref, gate_out)


def middle_kernel(recv_ref, stream_ref, gate_ref, wo_ref, kv_ref, wq_ref, wg_ref, out_ref, stream_out, gate_out):
    stream = finish_layer(0, recv_ref, stream_ref, gate_ref, wo_ref)
    stream_out[...] = stream
    begin_layer(1, stream, kv_ref, wq_ref, wg_ref, out_ref, gate_out)


def turn_kernel(level, recv_ref, stream_ref, gate_ref, wo_ref, kv_ref, wq_ref, wg_ref, emb_ref, table_ref,
                out_ref, stream_out, gate_out, logits_out):
    stream = finish_layer(1, recv_ref, stream_ref, gate_ref, wo_ref)
    logits_out[...] = level_logits(level - 1, stream, table_ref)
    stream = stream + emb_ref[level]
    stream_out[...] = stream
    begin_layer(0, stream, kv_ref, wq_ref, wg_ref, out_ref, gate_out)


def last_kernel(recv_ref, stream_ref, gate_ref, wo_ref, table_ref, *rest):
    early, logits_out = rest[:-1], rest[-1]
    stream = finish_layer(1, recv_ref, stream_ref, gate_ref, wo_ref)
    logits = jnp.concatenate(
        [ref[...] for ref in early] + [level_logits(LEVELS - 1, stream, table_ref)], axis=-1
    )
    logits_out[...] = jnp.broadcast_to(logits[None], (NQ, BEAMS, LEVELS * V))


VMEM = pl.BlockSpec(memory_space=pltpu.VMEM)


def call(kernel, args, outs):
    return pl.pallas_call(
        kernel,
        in_specs=[VMEM] * len(args),
        out_specs=[VMEM] * len(outs),
        out_shape=[jax.ShapeDtypeStruct(shape, kind) for shape, kind in outs],
        compiler_params=pltpu.CompilerParams(vmem_limit_bytes=32 * 1024 * 1024),
    )(*args)


STEP_OUTS = [((AREA * BEAMS, COLS), bf16), ((BEAMS, D), f32), ((BEAMS, D), f32)]


def body(
    kv_cache, spill_cache, spill_owner, lengths, beam_tokens, codebook_embed, w_query, w_gate, w_out
):
    ci, qi = lax.axis_index("core"), lax.axis_index("quad")
    li, yi = lax.axis_index("zl"), lax.axis_index("y")
    span = kv_cache.shape[1]
    spill = spill_cache.shape[1]

    table = lax.all_gather(codebook_embed, USER_AXES, axis=1, tiled=True)
    tokens = lax.all_gather(beam_tokens, "core", axis=0, tiled=True)

    positions = ((qi * NL + li) * NY + yi) * span + jnp.arange(span, dtype=jnp.int32)
    valid = positions[None, :] < lengths[:, None]
    owned = jnp.arange(U_DEV, dtype=jnp.int32) == spill_owner[0, 0]
    keep = jnp.concatenate([valid, jnp.broadcast_to(owned[:, None], (U_DEV, spill))], axis=1)
    resident = kv_cache.reshape(U_DEV, span, LAYERS, 2, NC, COLS)
    extra = jnp.broadcast_to(
        spill_cache.reshape(1, spill, LAYERS, 2, NC, COLS), (U_DEV, spill, LAYERS, 2, NC, COLS)
    )
    memory = jnp.concatenate([resident, extra], axis=1)
    is_value = jnp.arange(2) == 1
    memory = jnp.where(
        keep[:, :, None, None, None, None] | is_value[None, None, None, :, None, None],
        memory,
        jnp.zeros((), bf16),
    )
    memory = memory.transpose(4, 0, 2, 3, 1, 5)
    memory = lax.all_to_all(memory, "core", 0, 0, tiled=True)
    memory = memory.reshape(NQ, LAYERS, 2, span + spill, COLS)
    memory = lax.all_to_all(memory, Z_AXES, 0, 0, axis_index_groups=RINGS, tiled=True)

    mine = lax.dynamic_index_in_dim(tokens, qi, 0, keepdims=False)
    onehot = (mine.T[:, :, None] == jnp.arange(V, dtype=jnp.int32)[None, None, :]).astype(bf16)
    embeds = jnp.einsum("tbv,tvd->tbd", onehot, table, preferred_element_type=f32)
    wq = lax.dynamic_slice_in_dim(w_query, ci * COLS, COLS, 2)

    def exchange(parts):
        return lax.all_to_all(parts, AREA_AXES, 0, 0, tiled=True)

    early = []
    for level in range(LEVELS):
        if level == 0:
            parts, stream, gate = call(first_kernel, (embeds, memory, wq, w_gate), STEP_OUTS)
        else:
            parts, stream, gate, logits = call(
                functools.partial(turn_kernel, level),
                (recv, stream, gate, w_out, memory, wq, w_gate, embeds, table),
                STEP_OUTS + [((BEAMS, V), f32)],
            )
            early.append(logits)
        recv = exchange(parts)
        parts, stream, gate = call(
            middle_kernel, (recv, stream, gate, w_out, memory, wq, w_gate), STEP_OUTS
        )
        recv = exchange(parts)
    (logits,) = call(
        last_kernel, (recv, stream, gate, w_out, table, *early), [((NQ, BEAMS, LEVELS * V), f32)]
    )
    logits = lax.all_to_all(logits, Z_AXES, 0, 0, axis_index_groups=RINGS, tiled=True)
    logits = lax.dynamic_slice_in_dim(logits, ci * U_DEV, U_DEV, 0)
    return logits.reshape(U_DEV, BEAMS, LEVELS, V)


def solution(mesh):
    inner = Mesh(
        mesh.devices.reshape(NX, NC, NQ, NL, NY), ("x", "core", "quad", "zl", "y")
    )
    users, seq = ("x", "core"), ("quad", "zl", "y")
    in_specs = (
        P(users, seq, None, None, None),
        P(users, seq, None, None, None),
        P(users, seq),
        P(users),
        P(users, None, None),
        P(None, users, None),
        P(),
        P(),
        P(),
    )
    out_specs = P(users, None, None, None)
    return jax.shard_map(body, mesh=inner, in_specs=in_specs, out_specs=out_specs, check_vma=False)
```

time: 342 us -> 241 us (0.70)
  blocking collectives: 187 us -> 113 us
  local copies, waits for them, and re-layouts: 20.7 us -> 4.36 us
  starting transfers between devices: 36.7 us -> 21 us
  waiting for transfers between devices: 70.3 us -> 77.8 us
    all_gather x4 -> x1, blocking collectives: 102 us -> 1.8 us  [body(): tokens = lax.all_gather(beam_tokens, 'core', axis=0, tiled=True)]
    all_to_all x6 -> x9, blocking collectives: 85.5 us -> 111 us  [the longest x8 105 us: exchange(): return lax.all_to_all(parts, AREA_AXES, 0, 0, tiled=True)]
    all_to_all x5 -> x2, starting transfers between devices: 36.6 us -> 21 us  [the longest x1 13.9 us: body(): lax.all_to_all(memory, Z_AXES, 0, 0, axis_index_groups=RINGS, tiled=True)]
    all_gather x1, waiting for transfers between devices: 19.2 us -> 31.5 us  [body(): table = lax.all_gather(codebook_embed, USER_AXES, axis=1, tiled=True)]
    unnamed x48 -> x16, local copies, waits for them, and re-layouts: 8.14 us -> 1.31 us
    squeeze x5 -> x0, local copies, waits for them, and re-layouts: 6.47 us -> none  [the longest x1 2.21 us: body(): table[LEVELS - 1]]
    all_to_all x5 -> x2, waiting for transfers between devices: 50.5 us -> 45.6 us  [the longest x1 32.5 us: body(): lax.all_to_all(memory, Z_AXES, 0, 0, axis_index_groups=RINGS, tiled=True)]
  transfers between devices with their start and end apart: 6 -> 3, of which waited for: 5 -> 3; matrix products, arithmetic and copies ran while one was open for 2% -> 1% of each run, Pallas kernels for 0% -> 0%
where the time goes in v2:
time: 241 us; the launch traced here: 240 us
  blocking collectives  113 us (47%)
  waiting for transfers between devices  77.8 us (32%)
  starting transfers between devices  21 us (9%)
  between operations  14.2 us (6%)
  Pallas kernels  7.74 us (3%)
  local copies, waits for them, and re-layouts  4.36 us (2%)
    all_to_all x8, blocking collectives, exchange(): return lax.all_to_all(parts, AREA_AXES, 0, 0, tiled=True)  105 us
    all_to_all x1, waiting for transfers between devices, body(): lax.all_to_all(memory, Z_AXES, 0, 0, axis_index_groups=RINGS, tiled=True)  32.5 us
    all_gather x1, waiting for transfers between devices, body(): table = lax.all_gather(codebook_embed, USER_AXES, axis=1, tiled=True)  31.5 us
    all_to_all x1, starting transfers between devices, body(): lax.all_to_all(memory, Z_AXES, 0, 0, axis_index_groups=RINGS, tiled=True)  13.9 us
    all_to_all x1, waiting for transfers between devices, body(): lax.all_to_all(logits, Z_AXES, 0, 0, axis_index_groups=RINGS, tiled=True)  13.1 us
    pallas_call x9, Pallas kernels, call(): pl.pallas_call(kernel, in_specs=[VMEM] * len(args), out_specs=[VMEM] * le...  7.74 us
    all_to_all x1, starting transfers between devices, body(): lax.all_to_all(logits, Z_AXES, 0, 0, axis_index_groups=RINGS, tiled=True)  7.14 us
    all_to_all x1, blocking collectives, body(): memory = lax.all_to_all(memory, 'core', 0, 0, tiled=True)  5.84 us
  transfers between devices with their start and end apart: 3, of which 3 were waited for; matrix products, arithmetic and copies ran while one was open for 1% of the time, Pallas kernels for 0%

profile of v2, /device:TPU:6, one launch (start us, length us, event | category | flops | bytes accessed | tf_op | source)
XLA Modules:
  0.0 239.8 jit_solution(5617051708550595595)
XLA Ops:
  6.5 1.3 broadcast_in_dim.20
  10.2 5.8 %all_to_all.103 = bf16[2,2,2,2,192,256]{5,4,3,2,1,0:T(8,128)(2,1)} all-to-all(bf16[2,2,2,2,192,256]{5,4,3,2,1,0:T(8,128)(2,1)S(1)} %fusion), channel_id=1, replica_groups=mesh['x'=4,'core'=2,'quad'=4,'zl'=4,'y'=4] {'core'}, dimensions={0} | all-to-all | bytes 3145728 | tf_op jit(solution)/shard_map/all_to_all | solution.py:148
  16.1 13.9 %all-to-all-start.1 = ((bf16[4,2,2,192,256]{4,3,2,1,0:T(8,128)(2,1)}), bf16[4,2,2,192,256]{4,3,2,1,0:T(8,128)(2,1)S(1)}, u32[]{:S(2)}, u32[]{:S(2)}) async-start(bf16[4,2,2,192,256]{4,3,2,1,0:T(8,128)(2,1)} %bitcast.42), calls=%async_computation.1 | async-start | bytes 3145728 | tf_op jit(solution)/shard_map/all_to_all | solution.py:150
  30.7 1.8 all_gather.6
  32.5 31.5 %all-gather.2.cloned.1.call-done.table_ref = bf16[4,256,512]{2,1,0:T(8,128)(2,1)} async-done(((bf16[4,32,512]{2,1,0:T(8,128)(2,1)}), bf16[4,256,512]{2,1,0:T(8,128)(2,1)}) %all-gather.2.cloned.1.call-update) | async-done | bytes 1048592 | tf_op jit(solution)/shard_map/all_gather | solution.py:129
  64.0 1.5 fusion.1.emb_ref
  65.5 32.5 %all-to-all-done.1.kv_ref = bf16[4,2,2,192,256]{4,3,2,1,0:T(8,128)(2,1)S(1)} async-done(((bf16[4,2,2,192,256]{4,3,2,1,0:T(8,128)(2,1)}), bf16[4,2,2,192,256]{4,3,2,1,0:T(8,128)(2,1)S(1)}, u32[]{:S(2)}, u32[]{:S(2)}) %all-to-all-start.1) | async-done | bytes 1572896 | tf_op jit(solution)/shard_map/all_to_all | solution.py:150
  98.1 1.2 copy-done.1
  99.9 19.8 %all_to_all.104 = bf16[32,8,256]{2,1,0:T(8,128)(2,1)S(1)} all-to-all(bf16[32,8,256]{2,1,0:T(8,128)(2,1)S(1)} %bitcast.41), channel_id=1, replica_groups=mesh['x'=4,'core'=2,'quad'=4,'zl'=4,'y'=4] {'core','zl','y'}, dimensions={0} | all-to-all | bytes 262144 | tf_op jit(solution)/shard_map/all_to_all | solution.py:158
  119.7 0.9 shard_map.92
  120.5 12.2 %all_to_all.105 = bf16[32,8,256]{2,1,0:T(8,128)(2,1)S(1)} all-to-all(bf16[32,8,256]{2,1,0:T(8,128)(2,1)S(1)} %bitcast.38), channel_id=1, replica_groups=mesh['x'=4,'core'=2,'quad'=4,'zl'=4,'y'=4] {'core','zl','y'}, dimensions={0} | all-to-all | bytes 262144 | tf_op jit(solution)/shard_map/all_to_all | solution.py:158
  132.7 0.9 shard_map.93
  133.6 12.2 %all_to_all.106 = bf16[32,8,256]{2,1,0:T(8,128)(2,1)S(1)} all-to-all(bf16[32,8,256]{2,1,0:T(8,128)(2,1)S(1)} %bitcast.36), channel_id=1, replica_groups=mesh['x'=4,'core'=2,'quad'=4,'zl'=4,'y'=4] {'core','zl','y'}, dimensions={0} | all-to-all | bytes 262144 | tf_op jit(solution)/shard_map/all_to_all | solution.py:158
  145.8 0.9 shard_map.94
  146.6 12.2 %all_to_all.107 = bf16[32,8,256]{2,1,0:T(8,128)(2,1)S(1)} all-to-all(bf16[32,8,256]{2,1,0:T(8,128)(2,1)S(1)} %bitcast.39), channel_id=1, replica_groups=mesh['x'=4,'core'=2,'quad'=4,'zl'=4,'y'=4] {'core','zl','y'}, dimensions={0} | all-to-all | bytes 262144 | tf_op jit(solution)/shard_map/all_to_all | solution.py:158
  158.8 0.9 shard_map.95
  159.7 12.2 %all_to_all.108 = bf16[32,8,256]{2,1,0:T(8,128)(2,1)S(1)} all-to-all(bf16[32,8,256]{2,1,0:T(8,128)(2,1)S(1)} %bitcast.37), channel_id=1, replica_groups=mesh['x'=4,'core'=2,'quad'=4,'zl'=4,'y'=4] {'core','zl','y'}, dimensions={0} | all-to-all | bytes 262144 | tf_op jit(solution)/shard_map/all_to_all | solution.py:158
  172.7 12.2 %all_to_all.109 = bf16[32,8,256]{2,1,0:T(8,128)(2,1)S(1)} all-to-all(bf16[32,8,256]{2,1,0:T(8,128)(2,1)S(1)} %bitcast.40), channel_id=1, replica_groups=mesh['x'=4,'core'=2,'quad'=4,'zl'=4,'y'=4] {'core','zl','y'}, dimensions={0} | all-to-all | bytes 262144 | tf_op jit(solution)/shard_map/all_to_all | solution.py:158
  184.9 0.9 shard_map.97
  185.8 12.2 %all_to_all.110 = bf16[32,8,256]{2,1,0:T(8,128)(2,1)S(1)} all-to-all(bf16[32,8,256]{2,1,0:T(8,128)(2,1)S(1)} %bitcast.34), channel_id=1, replica_groups=mesh['x'=4,'core'=2,'quad'=4,'zl'=4,'y'=4] {'core','zl','y'}, dimensions={0} | all-to-all | bytes 262144 | tf_op jit(solution)/shard_map/all_to_all | solution.py:158
  198.8 12.2 %all_to_all.111 = bf16[32,8,256]{2,1,0:T(8,128)(2,1)S(1)} all-to-all(bf16[32,8,256]{2,1,0:T(8,128)(2,1)S(1)} %bitcast.35), channel_id=1, replica_groups=mesh['x'=4,'core'=2,'quad'=4,'zl'=4,'y'=4] {'core','zl','y'}, dimensions={0} | all-to-all | bytes 262144 | tf_op jit(solution)/shard_map/all_to_all | solution.py:158
  211.0 1.1 shard_map.99
  212.1 7.1 %all-to-all-start.10 = ((f32[4,8,1024]{2,1,0:T(8,128)}), f32[4,8,1024]{2,1,0:T(8,128)S(1)}, u32[]{:S(2)}, u32[]{:S(2)}) async-start(f32[4,8,1024]{2,1,0:T(8,128)} %shard_map.99), calls=%async_computation.10 | async-start | bytes 262144 | tf_op jit(solution)/shard_map/all_to_all | solution.py:179
  219.2 13.1 %all-to-all-done.10 = f32[4,8,1024]{2,1,0:T(8,128)S(1)} async-done(((f32[4,8,1024]{2,1,0:T(8,128)}), f32[4,8,1024]{2,1,0:T(8,128)S(1)}, u32[]{:S(2)}, u32[]{:S(2)}) %all-to-all-start.10) | async-done | bytes 131104 | tf_op jit(solution)/shard_map/all_to_all | solution.py:179
  (36 shorter events, 5.4 us)
Async XLA Ops:
  6.5 25.9 %copy-start = (bf16[2,512,512]{2,1,0:T(8,128)(2,1)S(1)}, bf16[2,512,512]{2,1,0:T(8,128)(2,1)}, u32[]{:S(2)}) copy-start(bf16[2,512,512]{2,1,0:T(8,128)(2,1)} %param.15) | copy-start | bytes 3145732
  6.5 1.4 copy-start.5
  8.6 0.9 copy-start.7
  16.0 14.6 %copy-start.6 = (s32[2,8,4]{1,2,0:T(4,128)S(1)}, s32[2,8,4]{1,2,0:T(4,128)}, u32[]{:S(2)}) copy-start(s32[2,8,4]{1,2,0:T(4,128)} %param.13) | copy-start | bytes 772
  16.1 82.0 %all-to-all-start.1 = ((bf16[4,2,2,192,256]{4,3,2,1,0:T(8,128)(2,1)}), bf16[4,2,2,192,256]{4,3,2,1,0:T(8,128)(2,1)S(1)}, u32[]{:S(2)}, u32[]{:S(2)}) async-start(bf16[4,2,2,192,256]{4,3,2,1,0:T(8,128)(2,1)} %bitcast.42), calls=%async_computation.1 | async-start | bytes 3145728 | tf_op jit(solution)/shard_map/all_to_all | solution.py:150
  29.9 34.1 %all-gather.2.cloned.1.call-start = ((), (), s32[]{:S(2)}) async-start(), calls=%async_computation.11 | async-start | bytes 1179648 | tf_op jit(solution)/shard_map/all_gather | solution.py:129
  98.1 1.2 copy-start.1
  99.3 20.4 %copy-start.2 = (bf16[2,512,512]{2,1,0:T(8,128)(2,1)S(1)}, bf16[2,512,512]{2,1,0:T(8,128)(2,1)}, u32[]{:S(2)}) copy-start(bf16[2,512,512]{2,1,0:T(8,128)(2,1)} %wg_ref.15) | copy-start | bytes 3145732
  99.3 20.4 %copy-start.3 = (bf16[2,512,512]{2,1,0:T(8,128)(2,1)S(1)}, bf16[2,512,512]{2,1,0:T(8,128)(2,1)}, u32[]{:S(2)}) copy-start(bf16[2,512,512]{2,1,0:T(8,128)(2,1)} %wo_ref.15) | copy-start | bytes 3145732
  119.7 13.0 %copy-start.4 = (bf16[4,256,512]{2,1,0:T(8,128)(2,1)S(1)}, bf16[4,256,512]{2,1,0:T(8,128)(2,1)}, u32[]{:S(2)}) copy-start(bf16[4,256,512]{2,1,0:T(8,128)(2,1)} %all-gather.2.cloned.1.call-done.table_ref) | copy-start | bytes 3145732
  212.1 20.2 %all-to-all-start.10 = ((f32[4,8,1024]{2,1,0:T(8,128)}), f32[4,8,1024]{2,1,0:T(8,128)S(1)}, u32[]{:S(2)}, u32[]{:S(2)}) async-start(f32[4,8,1024]{2,1,0:T(8,128)} %shard_map.99), calls=%async_computation.10 | async-start | bytes 262144 | tf_op jit(solution)/shard_map/all_to_all | solution.py:179
Sparse Core Ops, SparseCore 0:
  32.9 31.0 all-gather.1

commit v3 on v2

--- a/solution.py
+++ b/solution.py
@@ -48,7 +48,8 @@
 def begin_layer(layer, stream, kv_ref, wq_ref, wg_ref, out_ref, gate_out):
     normed = normalize(stream).astype(bf16)
     query = jnp.dot(normed, wq_ref[layer], preferred_element_type=f32)
-    gate_out[...] = silu(jnp.dot(normed, wg_ref[layer], preferred_element_type=f32))
+    if wg_ref is not None:
+        gate_out[...] = silu(jnp.dot(normed, wg_ref[layer], preferred_element_type=f32))
     head_of = lax.broadcasted_iota(jnp.int32, (BEAMS, COLS), 1) // HEAD
     spread = jnp.concatenate([jnp.where(head_of == h, query, 0.0) for h in range(HEADS)], axis=0)
     keys = kv_ref[:, layer, 0].reshape(-1, COLS)
@@ -72,10 +73,16 @@
     ) * D ** (-0.5)
 
 
-def first_kernel(emb_ref, kv_ref, wq_ref, wg_ref, out_ref, stream_out, gate_out):
+def gate_kernel(emb_ref, wg_ref, wo_ref, gate_out):
+    normed = normalize(emb_ref[0]).astype(bf16)
+    gate_out[...] = silu(jnp.dot(normed, wg_ref[0], preferred_element_type=f32))
+
+
+def first_kernel(emb_ref, gate_ref, kv_ref, wq_ref, out_ref, stream_out, gate_out):
     stream = emb_ref[0]
     stream_out[...] = stream
-    begin_layer(0, stream, kv_ref, wq_ref, wg_ref, out_ref, gate_out)
+    gate_out[...] = gate_ref[...]
+    begin_layer(0, stream, kv_ref, wq_ref, None, out_ref, None)
 
 
 def middle_kernel(recv_ref, stream_ref, gate_ref, wo_ref, kv_ref, wq_ref, wg_ref, out_ref, stream_out, gate_out):
@@ -99,7 +106,7 @@
     logits = jnp.concatenate(
         [ref[...] for ref in early] + [level_logits(LEVELS - 1, stream, table_ref)], axis=-1
     )
-    logits_out[...] = jnp.broadcast_to(logits[None], (NQ, BEAMS, LEVELS * V))
+    logits_out[...] = jnp.broadcast_to(logits[None], (NQ, BEAMS, LEVELS * V)).astype(bf16)
 
 
 VMEM = pl.BlockSpec(memory_space=pltpu.VMEM)
@@ -157,10 +164,11 @@
     def exchange(parts):
         return lax.all_to_all(parts, AREA_AXES, 0, 0, tiled=True)
 
+    (early_gate,) = call(gate_kernel, (embeds, w_gate, w_out), STEP_OUTS[2:])
     early = []
     for level in range(LEVELS):
         if level == 0:
-            parts, stream, gate = call(first_kernel, (embeds, memory, wq, w_gate), STEP_OUTS)
+            parts, stream, gate = call(first_kernel, (embeds, early_gate, memory, wq), STEP_OUTS)
         else:
             parts, stream, gate, logits = call(
                 functools.partial(turn_kernel, level),
@@ -174,11 +182,11 @@
         )
         recv = exchange(parts)
     (logits,) = call(
-        last_kernel, (recv, stream, gate, w_out, table, *early), [((NQ, BEAMS, LEVELS * V), f32)]
+        last_kernel, (recv, stream, gate, w_out, table, *early), [((NQ, BEAMS, LEVELS * V), bf16)]
     )
     logits = lax.all_to_all(logits, Z_AXES, 0, 0, axis_index_groups=RINGS, tiled=True)
     logits = lax.dynamic_slice_in_dim(logits, ci * U_DEV, U_DEV, 0)
-    return logits.reshape(U_DEV, BEAMS, LEVELS, V)
+    return logits.astype(f32).reshape(U_DEV, BEAMS, LEVELS, V)
 
 
 def solution(mesh):

time: 241 us -> 237 us (0.983)
  waiting for transfers between devices: 77.8 us -> 74 us
    pallas_call x9 -> x10, Pallas kernels: 7.74 us -> 7.94 us  [call(): pl.pallas_call(kernel, in_specs=[VMEM] * len(args), out_specs=[VMEM] * le...]
where the time goes in v3:
time: 237 us; the launch traced here: 236 us
  blocking collectives  113 us (48%)
  waiting for transfers between devices  74 us (31%)
  starting transfers between devices  21 us (9%)
  between operations  14.2 us (6%)
  Pallas kernels  7.94 us (3%)
  local copies, waits for them, and re-layouts  4.36 us (2%)
    all_to_all x8, blocking collectives, exchange(): return lax.all_to_all(parts, AREA_AXES, 0, 0, tiled=True)  105 us
    all_gather x1, waiting for transfers between devices, body(): table = lax.all_gather(codebook_embed, USER_AXES, axis=1, tiled=True)  31.5 us
    all_to_all x1, waiting for transfers between devices, body(): lax.all_to_all(memory, Z_AXES, 0, 0, axis_index_groups=RINGS, tiled=True)  30.9 us
    all_to_all x1, starting transfers between devices, body(): lax.all_to_all(memory, Z_AXES, 0, 0, axis_index_groups=RINGS, tiled=True)  13.9 us
    all_to_all x1, waiting for transfers between devices, body(): lax.all_to_all(logits, Z_AXES, 0, 0, axis_index_groups=RINGS, tiled=True)  10.8 us
    pallas_call x10, Pallas kernels, call(): pl.pallas_call(kernel, in_specs=[VMEM] * len(args), out_specs=[VMEM] * le...  7.94 us
    all_to_all x1, starting transfers between devices, body(): lax.all_to_all(logits, Z_AXES, 0, 0, axis_index_groups=RINGS, tiled=True)  7.14 us
    all_to_all x1, blocking collectives, body(): memory = lax.all_to_all(memory, 'core', 0, 0, tiled=True)  5.84 us
  transfers between devices with their start and end apart: 3, of which 3 were waited for; matrix products, arithmetic and copies ran while one was open for 1% of the time, Pallas kernels for 0%

profile of v3, /device:TPU:6, one launch (start us, length us, event | category | flops | bytes accessed | tf_op | source)
XLA Modules:
  0.0 236.3 jit_solution(3947867554120287543)
XLA Ops:
  6.5 1.3 broadcast_in_dim.20
  10.2 5.8 %all_to_all.103 = bf16[2,2,2,2,192,256]{5,4,3,2,1,0:T(8,128)(2,1)} all-to-all(bf16[2,2,2,2,192,256]{5,4,3,2,1,0:T(8,128)(2,1)S(1)} %fusion), channel_id=1, replica_groups=mesh['x'=4,'core'=2,'quad'=4,'zl'=4,'y'=4] {'core'}, dimensions={0} | all-to-all | bytes 3145728 | tf_op jit(solution)/shard_map/all_to_all | solution.py:155
  16.0 13.9 %all-to-all-start.1 = ((bf16[4,2,2,192,256]{4,3,2,1,0:T(8,128)(2,1)}), bf16[4,2,2,192,256]{4,3,2,1,0:T(8,128)(2,1)S(1)}, u32[]{:S(2)}, u32[]{:S(2)}) async-start(bf16[4,2,2,192,256]{4,3,2,1,0:T(8,128)(2,1)} %bitcast.44), calls=%async_computation.1 | async-start | bytes 3145728 | tf_op jit(solution)/shard_map/all_to_all | solution.py:157
  30.7 1.8 all_gather.6
  32.5 31.5 %all-gather.2.cloned.1.call-done.table_ref = bf16[4,256,512]{2,1,0:T(8,128)(2,1)} async-done(((bf16[4,32,512]{2,1,0:T(8,128)(2,1)}), bf16[4,256,512]{2,1,0:T(8,128)(2,1)}) %all-gather.2.cloned.1.call-update) | async-done | bytes 1048592 | tf_op jit(solution)/shard_map/all_gather | solution.py:136
  64.0 1.6 fusion.1.emb_ref
  65.6 1.2 copy-done.3
  67.1 30.9 %all-to-all-done.1.kv_ref = bf16[4,2,2,192,256]{4,3,2,1,0:T(8,128)(2,1)S(1)} async-done(((bf16[4,2,2,192,256]{4,3,2,1,0:T(8,128)(2,1)}), bf16[4,2,2,192,256]{4,3,2,1,0:T(8,128)(2,1)S(1)}, u32[]{:S(2)}, u32[]{:S(2)}) %all-to-all-start.1) | async-done | bytes 1572896 | tf_op jit(solution)/shard_map/all_to_all | solution.py:157
  98.6 19.8 %all_to_all.104 = bf16[32,8,256]{2,1,0:T(8,128)(2,1)S(1)} all-to-all(bf16[32,8,256]{2,1,0:T(8,128)(2,1)S(1)} %bitcast.43), channel_id=1, replica_groups=mesh['x'=4,'core'=2,'quad'=4,'zl'=4,'y'=4] {'core','zl','y'}, dimensions={0} | all-to-all | bytes 262144 | tf_op jit(solution)/shard_map/all_to_all | solution.py:165
  118.4 0.9 shard_map.93
  119.3 12.2 %all_to_all.105 = bf16[32,8,256]{2,1,0:T(8,128)(2,1)S(1)} all-to-all(bf16[32,8,256]{2,1,0:T(8,128)(2,1)S(1)} %bitcast.40), channel_id=1, replica_groups=mesh['x'=4,'core'=2,'quad'=4,'zl'=4,'y'=4] {'core','zl','y'}, dimensions={0} | all-to-all | bytes 262144 | tf_op jit(solution)/shard_map/all_to_all | solution.py:165
  131.5 0.9 shard_map.94
  132.4 12.2 %all_to_all.106 = bf16[32,8,256]{2,1,0:T(8,128)(2,1)S(1)} all-to-all(bf16[32,8,256]{2,1,0:T(8,128)(2,1)S(1)} %bitcast.38), channel_id=1, replica_groups=mesh['x'=4,'core'=2,'quad'=4,'zl'=4,'y'=4] {'core','zl','y'}, dimensions={0} | all-to-all | bytes 262144 | tf_op jit(solution)/shard_map/all_to_all | solution.py:165
  144.5 0.9 shard_map.95
  145.4 12.2 %all_to_all.107 = bf16[32,8,256]{2,1,0:T(8,128)(2,1)S(1)} all-to-all(bf16[32,8,256]{2,1,0:T(8,128)(2,1)S(1)} %bitcast.41), channel_id=1, replica_groups=mesh['x'=4,'core'=2,'quad'=4,'zl'=4,'y'=4] {'core','zl','y'}, dimensions={0} | all-to-all | bytes 262144 | tf_op jit(solution)/shard_map/all_to_all | solution.py:165
  157.6 0.9 shard_map.96
  158.4 12.2 %all_to_all.108 = bf16[32,8,256]{2,1,0:T(8,128)(2,1)S(1)} all-to-all(bf16[32,8,256]{2,1,0:T(8,128)(2,1)S(1)} %bitcast.39), channel_id=1, replica_groups=mesh['x'=4,'core'=2,'quad'=4,'zl'=4,'y'=4] {'core','zl','y'}, dimensions={0} | all-to-all | bytes 262144 | tf_op jit(solution)/shard_map/all_to_all | solution.py:165
  171.5 12.2 %all_to_all.109 = bf16[32,8,256]{2,1,0:T(8,128)(2,1)S(1)} all-to-all(bf16[32,8,256]{2,1,0:T(8,128)(2,1)S(1)} %bitcast.42), channel_id=1, replica_groups=mesh['x'=4,'core'=2,'quad'=4,'zl'=4,'y'=4] {'core','zl','y'}, dimensions={0} | all-to-all | bytes 262144 | tf_op jit(solution)/shard_map/all_to_all | solution.py:165
  183.6 0.9 shard_map.98
  184.5 12.2 %all_to_all.110 = bf16[32,8,256]{2,1,0:T(8,128)(2,1)S(1)} all-to-all(bf16[32,8,256]{2,1,0:T(8,128)(2,1)S(1)} %bitcast.36), channel_id=1, replica_groups=mesh['x'=4,'core'=2,'quad'=4,'zl'=4,'y'=4] {'core','zl','y'}, dimensions={0} | all-to-all | bytes 262144 | tf_op jit(solution)/shard_map/all_to_all | solution.py:165
  197.6 12.2 %all_to_all.111 = bf16[32,8,256]{2,1,0:T(8,128)(2,1)S(1)} all-to-all(bf16[32,8,256]{2,1,0:T(8,128)(2,1)S(1)} %bitcast.37), channel_id=1, replica_groups=mesh['x'=4,'core'=2,'quad'=4,'zl'=4,'y'=4] {'core','zl','y'}, dimensions={0} | all-to-all | bytes 262144 | tf_op jit(solution)/shard_map/all_to_all | solution.py:165
  209.7 1.1 shard_map.100
  210.8 7.1 %all-to-all-start.10 = ((bf16[4,8,1024]{2,1,0:T(8,128)(2,1)}), bf16[4,8,1024]{2,1,0:T(8,128)(2,1)S(1)}, u32[]{:S(2)}, u32[]{:S(2)}) async-start(bf16[4,8,1024]{2,1,0:T(8,128)(2,1)} %shard_map.100), calls=%async_computation.10 | async-start | bytes 131072 | tf_op jit(solution)/shard_map/all_to_all | solution.py:187
  218.0 10.8 %all-to-all-done.10 = bf16[4,8,1024]{2,1,0:T(8,128)(2,1)S(1)} async-done(((bf16[4,8,1024]{2,1,0:T(8,128)(2,1)}), bf16[4,8,1024]{2,1,0:T(8,128)(2,1)S(1)}, u32[]{:S(2)}, u32[]{:S(2)}) %all-to-all-start.10) | async-done | bytes 65568 | tf_op jit(solution)/shard_map/all_to_all | solution.py:187
  (39 shorter events, 5.6 us)
Async XLA Ops:
  6.5 25.9 %copy-start = (bf16[2,512,512]{2,1,0:T(8,128)(2,1)S(1)}, bf16[2,512,512]{2,1,0:T(8,128)(2,1)}, u32[]{:S(2)}) copy-start(bf16[2,512,512]{2,1,0:T(8,128)(2,1)} %param.15) | copy-start | bytes 3145732
  6.5 1.4 copy-start.6
  8.6 0.9 copy-start.8
  16.0 14.6 %copy-start.7 = (s32[2,8,4]{1,2,0:T(4,128)S(1)}, s32[2,8,4]{1,2,0:T(4,128)}, u32[]{:S(2)}) copy-start(s32[2,8,4]{1,2,0:T(4,128)} %param.13) | copy-start | bytes 772
  16.0 82.0 %all-to-all-start.1 = ((bf16[4,2,2,192,256]{4,3,2,1,0:T(8,128)(2,1)}), bf16[4,2,2,192,256]{4,3,2,1,0:T(8,128)(2,1)S(1)}, u32[]{:S(2)}, u32[]{:S(2)}) async-start(bf16[4,2,2,192,256]{4,3,2,1,0:T(8,128)(2,1)} %bitcast.44), calls=%async_computation.1 | async-start | bytes 3145728 | tf_op jit(solution)/shard_map/all_to_all | solution.py:157
  29.9 34.1 %all-gather.2.cloned.1.call-start = ((), (), s32[]{:S(2)}) async-start(), calls=%async_computation.11 | async-start | bytes 1179648 | tf_op jit(solution)/shard_map/all_gather | solution.py:136
  64.0 1.6 copy-start.1
  65.6 1.2 copy-start.3
  98.0 20.4 %copy-start.2 = (bf16[2,512,512]{2,1,0:T(8,128)(2,1)S(1)}, bf16[2,512,512]{2,1,0:T(8,128)(2,1)}, u32[]{:S(2)}) copy-start(bf16[2,512,512]{2,1,0:T(8,128)(2,1)} %wo_ref.17) | copy-start | bytes 3145732
  98.0 20.4 %copy-start.4 = (bf16[2,512,512]{2,1,0:T(8,128)(2,1)S(1)}, bf16[2,512,512]{2,1,0:T(8,128)(2,1)}, u32[]{:S(2)}) copy-start(bf16[2,512,512]{2,1,0:T(8,128)(2,1)} %wg_ref.15) | copy-start | bytes 3145732
  118.4 13.0 %copy-start.5 = (bf16[4,256,512]{2,1,0:T(8,128)(2,1)S(1)}, bf16[4,256,512]{2,1,0:T(8,128)(2,1)}, u32[]{:S(2)}) copy-start(bf16[4,256,512]{2,1,0:T(8,128)(2,1)} %all-gather.2.cloned.1.call-done.table_ref) | copy-start | bytes 3145732
  210.8 18.0 %all-to-all-start.10 = ((bf16[4,8,1024]{2,1,0:T(8,128)(2,1)}), bf16[4,8,1024]{2,1,0:T(8,128)(2,1)S(1)}, u32[]{:S(2)}, u32[]{:S(2)}) async-start(bf16[4,8,1024]{2,1,0:T(8,128)(2,1)} %shard_map.100), calls=%async_computation.10 | async-start | bytes 131072 | tf_op jit(solution)/shard_map/all_to_all | solution.py:187
Sparse Core Ops, SparseCore 0:
  32.9 31.0 all-gather.1

commit v4 on v3

--- a/solution.py
+++ b/solution.py
@@ -103,10 +103,9 @@
 def last_kernel(recv_ref, stream_ref, gate_ref, wo_ref, table_ref, *rest):
     early, logits_out = rest[:-1], rest[-1]
     stream = finish_layer(1, recv_ref, stream_ref, gate_ref, wo_ref)
-    logits = jnp.concatenate(
-        [ref[...] for ref in early] + [level_logits(LEVELS - 1, stream, table_ref)], axis=-1
-    )
-    logits_out[...] = jnp.broadcast_to(logits[None], (NQ, BEAMS, LEVELS * V)).astype(bf16)
+    levels = [ref[...] for ref in early] + [level_logits(LEVELS - 1, stream, table_ref)]
+    logits = jnp.stack(levels, axis=1)
+    logits_out[...] = jnp.broadcast_to(logits[None], (NQ, BEAMS, LEVELS, V)).astype(bf16)
 
 
 VMEM = pl.BlockSpec(memory_space=pltpu.VMEM)
@@ -182,11 +181,11 @@
         )
         recv = exchange(parts)
     (logits,) = call(
-        last_kernel, (recv, stream, gate, w_out, table, *early), [((NQ, BEAMS, LEVELS * V), bf16)]
+        last_kernel, (recv, stream, gate, w_out, table, *early), [((NQ, BEAMS, LEVELS, V), bf16)]
     )
     logits = lax.all_to_all(logits, Z_AXES, 0, 0, axis_index_groups=RINGS, tiled=True)
     logits = lax.dynamic_slice_in_dim(logits, ci * U_DEV, U_DEV, 0)
-    return logits.astype(f32).reshape(U_DEV, BEAMS, LEVELS, V)
+    return logits.astype(f32)
 
 
 def solution(mesh):

time: 237 us -> 242 us (1.021)
  local copies, waits for them, and re-layouts: 4.36 us -> 7.46 us
    reshape x2, local copies, waits for them, and re-layouts: 0.91 us -> 4.77 us  [body(): resident = kv_cache.reshape(U_DEV, span, LAYERS, 2, NC, COLS)]
where the time goes in v4:
time: 242 us; the launch traced here: 241 us
  blocking collectives  113 us (47%)
  waiting for transfers between devices  74 us (31%)
  starting transfers between devices  21 us (9%)
  between operations  14.2 us (6%)
  Pallas kernels  7.96 us (3%)
  local copies, waits for them, and re-layouts  7.46 us (3%)
    all_to_all x8, blocking collectives, exchange(): return lax.all_to_all(parts, AREA_AXES, 0, 0, tiled=True)  105 us
    all_gather x1, waiting for transfers between devices, body(): table = lax.all_gather(codebook_embed, USER_AXES, axis=1, tiled=True)  31.5 us
    all_to_all x1, waiting for transfers between devices, body(): lax.all_to_all(memory, Z_AXES, 0, 0, axis_index_groups=RINGS, tiled=True)  30.9 us
    all_to_all x1, starting transfers between devices, body(): lax.all_to_all(memory, Z_AXES, 0, 0, axis_index_groups=RINGS, tiled=True)  13.9 us
    all_to_all x1, waiting for transfers between devices, body(): lax.all_to_all(logits, Z_AXES, 0, 0, axis_index_groups=RINGS, tiled=True)  10.8 us
    pallas_call x10, Pallas kernels, call(): pl.pallas_call(kernel, in_specs=[VMEM] * len(args), out_specs=[VMEM] * le...  7.96 us
    all_to_all x1, starting transfers between devices, body(): lax.all_to_all(logits, Z_AXES, 0, 0, axis_index_groups=RINGS, tiled=True)  7.14 us
    all_to_all x1, blocking collectives, body(): memory = lax.all_to_all(memory, 'core', 0, 0, tiled=True)  5.84 us
  transfers between devices with their start and end apart: 3, of which 3 were waited for; matrix products, arithmetic and copies ran while one was open for 1% of the time, Pallas kernels for 0%

profile of v4, /device:TPU:6, one launch (start us, length us, event | category | flops | bytes accessed | tf_op | source)
XLA Modules:
  0.0 241.3 jit_solution(11939757734839489361)
XLA Ops:
  6.5 1.2 broadcast_in_dim.20
  7.8 3.5 %reshape.45 = bf16[2,128,2,2,2,256]{5,4,3,2,1,0:T(2,128)(2,1)S(1)} reshape(bf16[2,128,2,2,512]{4,3,2,1,0:T(2,128)(2,1)} %param.9) | data formatting | bytes 2097152 | tf_op jit(solution)/shard_map/reshape | solution.py:142
  11.4 1.2 copy.13
  13.6 1.6 fusion
  15.2 5.8 %all_to_all.103 = bf16[2,2,2,2,192,256]{5,4,3,2,1,0:T(8,128)(2,1)} all-to-all(bf16[2,2,2,2,192,256]{5,4,3,2,1,0:T(8,128)(2,1)S(1)} %fusion), channel_id=1, replica_groups=mesh['x'=4,'core'=2,'quad'=4,'zl'=4,'y'=4] {'core'}, dimensions={0} | all-to-all | bytes 3145728 | tf_op jit(solution)/shard_map/all_to_all | solution.py:154
  21.0 13.9 %all-to-all-start.1 = ((bf16[4,2,2,192,256]{4,3,2,1,0:T(8,128)(2,1)}), bf16[4,2,2,192,256]{4,3,2,1,0:T(8,128)(2,1)S(1)}, u32[]{:S(2)}, u32[]{:S(2)}) async-start(bf16[4,2,2,192,256]{4,3,2,1,0:T(8,128)(2,1)} %bitcast.42), calls=%async_computation.1 | async-start | bytes 3145728 | tf_op jit(solution)/shard_map/all_to_all | solution.py:156
  35.6 1.8 all_gather.6
  37.5 31.5 %all-gather.2.cloned.1.call-done.table_ref = bf16[4,256,512]{2,1,0:T(8,128)(2,1)} async-done(((bf16[4,32,512]{2,1,0:T(8,128)(2,1)}), bf16[4,256,512]{2,1,0:T(8,128)(2,1)}) %all-gather.2.cloned.1.call-update) | async-done | bytes 1048592 | tf_op jit(solution)/shard_map/all_gather | solution.py:135
  69.0 1.6 fusion.1.emb_ref
  70.6 1.2 copy-done.3
  72.1 30.9 %all-to-all-done.1.kv_ref = bf16[4,2,2,192,256]{4,3,2,1,0:T(8,128)(2,1)S(1)} async-done(((bf16[4,2,2,192,256]{4,3,2,1,0:T(8,128)(2,1)}), bf16[4,2,2,192,256]{4,3,2,1,0:T(8,128)(2,1)S(1)}, u32[]{:S(2)}, u32[]{:S(2)}) %all-to-all-start.1) | async-done | bytes 1572896 | tf_op jit(solution)/shard_map/all_to_all | solution.py:156
  103.6 19.8 %all_to_all.104 = bf16[32,8,256]{2,1,0:T(8,128)(2,1)S(1)} all-to-all(bf16[32,8,256]{2,1,0:T(8,128)(2,1)S(1)} %bitcast.41), channel_id=1, replica_groups=mesh['x'=4,'core'=2,'quad'=4,'zl'=4,'y'=4] {'core','zl','y'}, dimensions={0} | all-to-all | bytes 262144 | tf_op jit(solution)/shard_map/all_to_all | solution.py:164
  124.2 12.2 %all_to_all.105 = bf16[32,8,256]{2,1,0:T(8,128)(2,1)S(1)} all-to-all(bf16[32,8,256]{2,1,0:T(8,128)(2,1)S(1)} %bitcast.38), channel_id=1, replica_groups=mesh['x'=4,'core'=2,'quad'=4,'zl'=4,'y'=4] {'core','zl','y'}, dimensions={0} | all-to-all | bytes 262144 | tf_op jit(solution)/shard_map/all_to_all | solution.py:164
  136.4 0.9 shard_map.94
  137.3 12.2 %all_to_all.106 = bf16[32,8,256]{2,1,0:T(8,128)(2,1)S(1)} all-to-all(bf16[32,8,256]{2,1,0:T(8,128)(2,1)S(1)} %bitcast.36), channel_id=1, replica_groups=mesh['x'=4,'core'=2,'quad'=4,'zl'=4,'y'=4] {'core','zl','y'}, dimensions={0} | all-to-all | bytes 262144 | tf_op jit(solution)/shard_map/all_to_all | solution.py:164
  150.3 12.2 %all_to_all.107 = bf16[32,8,256]{2,1,0:T(8,128)(2,1)S(1)} all-to-all(bf16[32,8,256]{2,1,0:T(8,128)(2,1)S(1)} %bitcast.39), channel_id=1, replica_groups=mesh['x'=4,'core'=2,'quad'=4,'zl'=4,'y'=4] {'core','zl','y'}, dimensions={0} | all-to-all | bytes 262144 | tf_op jit(solution)/shard_map/all_to_all | solution.py:164
  162.5 0.9 shard_map.96
  163.4 12.2 %all_to_all.108 = bf16[32,8,256]{2,1,0:T(8,128)(2,1)S(1)} all-to-all(bf16[32,8,256]{2,1,0:T(8,128)(2,1)S(1)} %bitcast.37), channel_id=1, replica_groups=mesh['x'=4,'core'=2,'quad'=4,'zl'=4,'y'=4] {'core','zl','y'}, dimensions={0} | all-to-all | bytes 262144 | tf_op jit(solution)/shard_map/all_to_all | solution.py:164
  176.4 12.2 %all_to_all.109 = bf16[32,8,256]{2,1,0:T(8,128)(2,1)S(1)} all-to-all(bf16[32,8,256]{2,1,0:T(8,128)(2,1)S(1)} %bitcast.40), channel_id=1, replica_groups=mesh['x'=4,'core'=2,'quad'=4,'zl'=4,'y'=4] {'core','zl','y'}, dimensions={0} | all-to-all | bytes 262144 | tf_op jit(solution)/shard_map/all_to_all | solution.py:164
  189.5 12.2 %all_to_all.110 = bf16[32,8,256]{2,1,0:T(8,128)(2,1)S(1)} all-to-all(bf16[32,8,256]{2,1,0:T(8,128)(2,1)S(1)} %bitcast.34), channel_id=1, replica_groups=mesh['x'=4,'core'=2,'quad'=4,'zl'=4,'y'=4] {'core','zl','y'}, dimensions={0} | all-to-all | bytes 262144 | tf_op jit(solution)/shard_map/all_to_all | solution.py:164
  202.5 12.2 %all_to_all.111 = bf16[32,8,256]{2,1,0:T(8,128)(2,1)S(1)} all-to-all(bf16[32,8,256]{2,1,0:T(8,128)(2,1)S(1)} %bitcast.35), channel_id=1, replica_groups=mesh['x'=4,'core'=2,'quad'=4,'zl'=4,'y'=4] {'core','zl','y'}, dimensions={0} | all-to-all | bytes 262144 | tf_op jit(solution)/shard_map/all_to_all | solution.py:164
  214.7 1.1 shard_map.100
  215.8 7.1 %all-to-all-start.10 = ((bf16[4,8,4,256]{3,2,1,0:T(4,128)(2,1)}), bf16[4,8,4,256]{3,2,1,0:T(4,128)(2,1)S(1)}, u32[]{:S(2)}, u32[]{:S(2)}) async-start(bf16[4,8,4,256]{3,2,1,0:T(4,128)(2,1)} %shard_map.100), calls=%async_computation.10 | async-start | bytes 131072 | tf_op jit(solution)/shard_map/all_to_all | solution.py:186
  222.9 10.8 %all-to-all-done.10 = bf16[4,8,4,256]{3,2,1,0:T(4,128)(2,1)S(1)} async-done(((bf16[4,8,4,256]{3,2,1,0:T(4,128)(2,1)}), bf16[4,8,4,256]{3,2,1,0:T(4,128)(2,1)S(1)}, u32[]{:S(2)}, u32[]{:S(2)}) %all-to-all-start.10) | async-done | bytes 65568 | tf_op jit(solution)/shard_map/all_to_all | solution.py:186
  (36 shorter events, 6.9 us)
Async XLA Ops:
  6.5 30.9 %copy-start = (bf16[2,512,512]{2,1,0:T(8,128)(2,1)S(1)}, bf16[2,512,512]{2,1,0:T(8,128)(2,1)}, u32[]{:S(2)}) copy-start(bf16[2,512,512]{2,1,0:T(8,128)(2,1)} %param.15) | copy-start | bytes 3145732
  11.4 1.9 copy-start.7
  21.0 14.6 %copy-start.6 = (s32[2,8,4]{1,2,0:T(4,128)S(1)}, s32[2,8,4]{1,2,0:T(4,128)}, u32[]{:S(2)}) copy-start(s32[2,8,4]{1,2,0:T(4,128)} %param.13) | copy-start | bytes 772
  21.0 82.0 %all-to-all-start.1 = ((bf16[4,2,2,192,256]{4,3,2,1,0:T(8,128)(2,1)}), bf16[4,2,2,192,256]{4,3,2,1,0:T(8,128)(2,1)S(1)}, u32[]{:S(2)}, u32[]{:S(2)}) async-start(bf16[4,2,2,192,256]{4,3,2,1,0:T(8,128)(2,1)} %bitcast.42), calls=%async_computation.1 | async-start | bytes 3145728 | tf_op jit(solution)/shard_map/all_to_all | solution.py:156
  34.9 34.1 %all-gather.2.cloned.1.call-start = ((), (), s32[]{:S(2)}) async-start(), calls=%async_computation.11 | async-start | bytes 1179648 | tf_op jit(solution)/shard_map/all_gather | solution.py:135
  69.0 1.6 copy-start.1
  70.6 1.2 copy-start.3
  103.0 20.4 %copy-start.2 = (bf16[2,512,512]{2,1,0:T(8,128)(2,1)S(1)}, bf16[2,512,512]{2,1,0:T(8,128)(2,1)}, u32[]{:S(2)}) copy-start(bf16[2,512,512]{2,1,0:T(8,128)(2,1)} %wo_ref.17) | copy-start | bytes 3145732
  103.0 20.4 %copy-start.4 = (bf16[2,512,512]{2,1,0:T(8,128)(2,1)S(1)}, bf16[2,512,512]{2,1,0:T(8,128)(2,1)}, u32[]{:S(2)}) copy-start(bf16[2,512,512]{2,1,0:T(8,128)(2,1)} %wg_ref.15) | copy-start | bytes 3145732
  123.4 13.0 %copy-start.5 = (bf16[4,256,512]{2,1,0:T(8,128)(2,1)S(1)}, bf16[4,256,512]{2,1,0:T(8,128)(2,1)}, u32[]{:S(2)}) copy-start(bf16[4,256,512]{2,1,0:T(8,128)(2,1)} %all-gather.2.cloned.1.call-done.table_ref) | copy-start | bytes 3145732
  215.8 18.0 %all-to-all-start.10 = ((bf16[4,8,4,256]{3,2,1,0:T(4,128)(2,1)}), bf16[4,8,4,256]{3,2,1,0:T(4,128)(2,1)S(1)}, u32[]{:S(2)}, u32[]{:S(2)}) async-start(bf16[4,8,4,256]{3,2,1,0:T(4,128)(2,1)} %shard_map.100), calls=%async_computation.10 | async-start | bytes 131072 | tf_op jit(solution)/shard_map/all_to_all | solution.py:186
Sparse Core Ops, SparseCore 0:
  37.8 31.0 all-gather.1
